TPU v7x, 32 devices: a whole 2x2x4 slice. The times are simulated.
32 devices in a mesh: groups: 2 (over x), owner: 16 (over z, y, core).
Axes of the slice: x: 2, y: 2, z: 4, core: 2. Of those that a mesh axis runs over, the one named last changes fastest.
Arguments:
- queries: bfloat16 [512, 8192], P(('groups', 'owner')), parts along dimension 0, may hold values from -12 to 12
- request_prefix: int32 [512, 1], P(('groups', 'owner')), parts along dimension 0, may hold values from 0 to 15; in each aligned block of 16 rows (0 to 15, 16 to 31, ...) at most 2 rows name the same one
- suffix_len: int32 [512], P(('groups', 'owner')), parts along dimension 0, may hold values from 1 to 32, 4096 in all
- block_map: int32 [64], P('groups'), parts along dimension 0, may hold values from 0 to 31, each once
- prefix_keys: bfloat16 [64, 1024, 1024], P(('groups', 'owner')), parts along dimension 0, may hold values from -12 to 12
- prefix_values: bfloat16 [64, 1024, 1024], P(('groups', 'owner')), parts along dimension 0, may hold values from -10 to 10
- suffix_keys: bfloat16 [512, 32, 1024], P(('groups', 'owner')), parts along dimension 0, may hold values from -12 to 12
- suffix_values: bfloat16 [512, 32, 1024], P(('groups', 'owner')), parts along dimension 0, may hold values from -10 to 10
Outputs:
- attended: bfloat16 [512, 8192], P(('groups', 'owner')), parts along dimension 0
There are 2 independent parts, one for each index of `groups`. A program takes and returns all parts, laid end to end along the dimension named above; each array names one. Nothing has to cross between parts.
Inputs may be any that keep to these rules, and one draw needn't show every extreme that they name: `request_prefix`: at most 2 requests of one device continue the same prefix. `block_map`: each slot appears once; slot s lies on owner s // 2.
All inputs are finite; a program needn't handle non-finite values. No bound on the sum of `suffix_len` on one device may be relied on, other than what follows from the above.
Results may differ from a plain program's by a relative error of at most 0.0043.
Values may be sent and summed in bfloat16 or wider, within the bound.
A program may use at most 128 MiB of HBM per device.

v0:
```python
import math

import jax
import jax.numpy as jnp
from jax import lax
from jax.sharding import PartitionSpec as P

HEADS = 64
KV_HEADS = 8
HEAD_DIM = 128
PREFIXES = 16
CAP = 2


NEG_FILL = -1e30


def span_terms(rows, span_keys, span_values):
    row_count = rows.shape[0]
    per_group = HEADS // KV_HEADS
    factor = 1.0 / math.sqrt(HEAD_DIM)
    query_heads = rows.reshape(row_count, KV_HEADS, per_group, HEAD_DIM)
    key_heads = span_keys.reshape(span_keys.shape[0], KV_HEADS, HEAD_DIM)
    value_heads = span_values.reshape(span_values.shape[0], KV_HEADS, HEAD_DIM)
    out_list = []
    lse_list = []
    for kv_head in range(KV_HEADS):
        scores = (
            jnp.einsum(
                "rgd,td->rgt",
                query_heads[:, kv_head],
                key_heads[:, kv_head],
                preferred_element_type=jnp.float32,
            )
            * factor
        )
        highest = jnp.max(scores, axis=-1, keepdims=True)
        expon = jnp.exp(scores - highest)
        summed = jnp.sum(expon, axis=-1)
        weights = expon.astype(jnp.bfloat16)
        mixed = (
            jnp.einsum(
                "rgt,td->rgd", weights, value_heads[:, kv_head], preferred_element_type=jnp.float32
            )
            / summed[..., None]
        )
        out_list.append(mixed.astype(jnp.bfloat16))
        lse_list.append(highest[..., 0] + jnp.log(summed))
    span_out = jnp.stack(out_list, axis=1).reshape(row_count, HEADS * HEAD_DIM)
    span_lse = jnp.stack(lse_list, axis=1).reshape(row_count, HEADS)
    return (span_out, span_lse)


def attend_rows(received, prefix_keys, prefix_values):
    sources, local_slots, item_count, row_width = received.shape
    out_list = []
    lse_list = []
    for slot_index in range(local_slots):
        rows = received[:, slot_index].reshape(sources * item_count, row_width)
        span_out, span_lse = span_terms(rows, prefix_keys[slot_index], prefix_values[slot_index])
        out_list.append(span_out.reshape(sources, item_count, row_width))
        lse_list.append(span_lse.reshape(sources, item_count, HEADS))
    return (jnp.stack(out_list, axis=1), jnp.stack(lse_list, axis=1))


def suffix_terms(queries, suffix_keys, suffix_values, suffix_len):
    row_count = queries.shape[0]
    suffix_room = suffix_keys.shape[1]
    per_group = HEADS // KV_HEADS
    factor = 1.0 / math.sqrt(HEAD_DIM)
    query_heads = queries.reshape(row_count, KV_HEADS, per_group, HEAD_DIM)
    key_heads = suffix_keys.reshape(row_count, suffix_room, KV_HEADS, HEAD_DIM)
    value_heads = suffix_values.reshape(row_count, suffix_room, KV_HEADS, HEAD_DIM)
    scores = (
        jnp.einsum("rhgd,rthd->rhgt", query_heads, key_heads, preferred_element_type=jnp.float32)
        * factor
    )
    visible = (jnp.arange(suffix_room, dtype=jnp.int32)[None, :] < suffix_len[:, None])[
        :, None, None, :
    ]
    highest = jnp.max(jnp.where(visible, scores, NEG_FILL), axis=-1, keepdims=True)
    expon = jnp.where(visible, jnp.exp(scores - highest), 0.0)
    summed = jnp.sum(expon, axis=-1)
    weights = expon.astype(jnp.bfloat16)
    mixed = (
        jnp.einsum("rhgt,rthd->rhgd", weights, value_heads, preferred_element_type=jnp.float32)
        / summed[..., None]
    )
    suffix_out = mixed.reshape(row_count, HEADS, HEAD_DIM)
    suffix_lse = (highest[..., 0] + jnp.log(summed)).reshape(row_count, HEADS)
    return (suffix_out, suffix_lse)


def combine_terms(span_out, span_lse, suffix_out, suffix_lse):
    row_count = span_out.shape[0]
    highest = jnp.maximum(jnp.max(span_lse, axis=1), suffix_lse)
    span_scale = jnp.exp(span_lse - highest[:, None, :])
    suffix_scale = jnp.exp(suffix_lse - highest)
    numerator = (
        jnp.sum(span_scale[..., None] * span_out.astype(jnp.float32), axis=1)
        + suffix_scale[..., None] * suffix_out
    )
    denominator = jnp.sum(span_scale, axis=1) + suffix_scale
    return (
        (numerator / denominator[..., None])
        .astype(jnp.bfloat16)
        .reshape(row_count, HEADS * HEAD_DIM)
    )


def body(
    queries,
    request_prefix,
    suffix_len,
    block_map,
    prefix_keys,
    prefix_values,
    suffix_keys,
    suffix_values,
):
    owners = lax.axis_size("owner")
    local_rows = queries.shape[0]
    row_width = queries.shape[1]
    slot_count = block_map.shape[0]
    local_slots = prefix_keys.shape[0]
    per_prefix = slot_count // PREFIXES
    slot_range = jnp.arange(slot_count, dtype=jnp.int32)
    prefix_ids = request_prefix[:, 0]
    span_ids = prefix_ids[:, None] * per_prefix + jnp.arange(per_prefix, dtype=jnp.int32)[None, :]
    table_match = span_ids[:, :, None] == slot_range[None, None, :]
    slot_of = jnp.sum(jnp.where(table_match, block_map[None, None, :], 0), axis=-1)
    row_order = jnp.arange(local_rows, dtype=jnp.int32)
    earlier = (prefix_ids[:, None] == prefix_ids[None, :]) & (
        row_order[None, :] < row_order[:, None]
    )
    row_rank = jnp.sum(earlier.astype(jnp.int32), axis=1)
    position = slot_of * CAP + row_rank[:, None]
    buffer_match = (
        position[:, :, None] == jnp.arange(slot_count * CAP, dtype=jnp.int32)[None, None, :]
    )
    picker = jnp.any(buffer_match, axis=1).astype(jnp.bfloat16)
    outgoing = jnp.einsum("ib,id->bd", picker, queries, preferred_element_type=jnp.float32).astype(
        jnp.bfloat16
    )
    outgoing = outgoing.reshape(owners, local_slots, CAP, row_width)
    part_out, part_lse = attend_rows(
        lax.all_to_all(outgoing, "owner", split_axis=0, concat_axis=0, tiled=True),
        prefix_keys,
        prefix_values,
    )
    back_out = lax.all_to_all(part_out, "owner", split_axis=0, concat_axis=0, tiled=True)
    back_lse = lax.all_to_all(part_lse, "owner", split_axis=0, concat_axis=0, tiled=True)
    flat_out = back_out.reshape(slot_count * CAP, row_width)
    flat_lse = back_lse.reshape(slot_count * CAP, HEADS)
    flat_index = position.reshape(-1)
    span_out = jnp.take(flat_out, flat_index, axis=0).reshape(
        local_rows, per_prefix, HEADS, HEAD_DIM
    )
    span_lse = jnp.take(flat_lse, flat_index, axis=0).reshape(local_rows, per_prefix, HEADS)
    suffix_out, suffix_lse = suffix_terms(queries, suffix_keys, suffix_values, suffix_len)
    return combine_terms(span_out, span_lse, suffix_out, suffix_lse)


def solution(mesh):
    placed = (
        P(("groups", "owner"), None),
        P(("groups", "owner"), None),
        P(("groups", "owner")),
        P("groups"),
        P(("groups", "owner"), None, None),
        P(("groups", "owner"), None, None),
        P(("groups", "owner"), None, None),
        P(("groups", "owner"), None, None),
    )
    return jax.shard_map(
        body, mesh=mesh, in_specs=placed, out_specs=P(("groups", "owner"), None), check_vma=False
    )
```

profile of v0, /device:TPU:0, one launch (start us, length us, event | category | flops | bytes accessed | tf_op | source)
XLA Modules:
  0.0 132.6 jit_solution(5191109495947289585)
XLA Ops:
  2.6 1.4 %convolution_convert_fusion = bf16[64,8192]{1,0:T(8,128)(2,1)S(1)} fusion(pred[16,64]{1,0:T(8,128)(4,1)S(1)} %fusion.124, bf16[16,8192]{1,0:T(8,128)(2,1)} %param.8), kind=kOutput, calls=%fused_computation.2 | convolution fusion | flops 17301504 | bytes 1311744 | tf_op jit(solution)/shard_map/ib,id->bd/dot_general | solution.py:142
  4.0 1.5 %reshape.484 = bf16[16,2,2,8192]{3,2,1,0:T(2,128)(2,1)} reshape(bf16[64,8192]{1,0:T(8,128)(2,1)S(1)} %convolution_convert_fusion) | data formatting | bytes 2097152 | tf_op jit(solution)/shard_map/reshape | solution.py:145
  5.5 7.4 %all-to-all-start = ((bf16[16,2,2,8192]{3,2,1,0:T(2,128)(2,1)}), bf16[16,2,2,8192]{3,2,1,0:T(2,128)(2,1)}, u32[]{:S(2)}, u32[]{:S(2)}) async-start(bf16[16,2,2,8192]{3,2,1,0:T(2,128)(2,1)} %reshape.484), calls=%async_computation | async-start | bytes 2097152 | tf_op jit(solution)/shard_map/all_to_all | solution.py:147
  13.1 4.0 %fusion.132 = (bf16[1,1024,1024]{2,1,0:T(8,128)(2,1)S(1)}, bf16[1,1024,1024]{2,1,0:T(8,128)(2,1)}) fusion(bf16[2,1024,1024]{2,1,0:T(8,128)(2,1)} %param.12), kind=kLoop, calls=%fused_computation.256 | loop fusion | bytes 8388608 | tf_op jit(solution)/shard_map/slice | solution.py:60
  17.1 2.6 %copy.316 = bf16[1,1024,1024]{1,2,0:T(8,128)(2,1)} copy(bf16[1,1024,1024]{2,1,0:T(8,128)(2,1)S(1)} %get-tuple-element.13) | data formatting | bytes 4194304
  19.6 4.0 %fusion.131 = (bf16[1,1024,1024]{2,1,0:T(8,128)(2,1)S(1)}, bf16[1,1024,1024]{2,1,0:T(8,128)(2,1)}) fusion(bf16[2,1024,1024]{2,1,0:T(8,128)(2,1)} %param.13), kind=kLoop, calls=%fused_computation.255 | loop fusion | bytes 8388608 | tf_op jit(solution)/shard_map/slice | solution.py:60
  23.6 2.6 %copy.349 = bf16[1,1024,1024]{1,2,0:T(8,128)(2,1)} copy(bf16[1,1024,1024]{2,1,0:T(8,128)(2,1)S(1)} %get-tuple-element.11) | data formatting | bytes 4194304
  26.2 2.9 %copy.333 = bf16[1,1024,1024]{1,2,0:T(8,128)(2,1)S(1)} copy(bf16[1,1024,1024]{2,1,0:T(8,128)(2,1)} %get-tuple-element.14) | data formatting | bytes 4194304
  29.1 4.0 %copy.358 = bf16[1,1024,1024]{1,2,0:T(8,128)(2,1)} copy(bf16[1,1024,1024]{2,1,0:T(8,128)(2,1)} %get-tuple-element.12) | data formatting | bytes 4194304
  36.0 3.5 %fusion.133 = (bf16[16,1,2,8192]{3,2,1,0:T(2,128)(2,1)}, bf16[16,1,2,8192]{3,2,1,0:T(2,128)(2,1)}) fusion(bf16[16,2,2,8192]{3,2,1,0:T(2,128)(2,1)} %all-to-all-done), kind=kLoop, calls=%fused_computation.257 | loop fusion | bytes 2097152 | tf_op jit(solution)/shard_map/slice | solution.py:59
  39.4 2.2 %reshape_reshape_squeeze.6 = bf16[32,8,8,128]{3,2,1,0:T(8,128)(2,1)} reshape(bf16[16,1,2,8192]{3,2,1,0:T(2,128)(2,1)} %get-tuple-element.15) | data formatting | bytes 1048576 | tf_op jit(solution)/shard_map/reshape;reshape;squeeze | solution.py:22
  41.6 2.4 %fusion.142 = (f32[32,8]{1,0:T(8,128)S(1)}, f32[32,8,1024]{2,1,0:T(8,128)}) fusion(bf16[1024,8,128]{0,2,1:T(8,128)(2,1)} %bitcast.468, bf16[32,8,8,128]{3,2,1,0:T(8,128)(2,1)} %reshape_reshape_squeeze.6), kind=kOutput, calls=%fused_computation.266 | convolution fusion | flops 67632896 | bytes 1377280 | tf_op jit(solution)/shard_map/rgd,td->rgt/dot_general | solution.py:29
  44.0 2.3 %fusion.143 = (f32[32,8]{1,0:T(8,128)S(1)}, f32[32,8,1024]{2,1,0:T(8,128)}) fusion(bf16[1024,8,128]{0,2,1:T(8,128)(2,1)} %bitcast.469, bf16[32,8,8,128]{3,2,1,0:T(8,128)(2,1)} %reshape_reshape_squeeze.6), kind=kOutput, calls=%fused_computation.267 | convolution fusion | flops 67632896 | bytes 1377280 | tf_op jit(solution)/shard_map/rgd,td->rgt/dot_general | solution.py:29
  46.4 1.3 fusion.144
  47.7 1.3 fusion.145
  49.0 1.3 fusion.146
  51.6 1.3 fusion.148
  54.1 2.3 %reshape_reshape_squeeze.7 = bf16[32,8,8,128]{3,2,1,0:T(8,128)(2,1)} reshape(bf16[16,1,2,8192]{3,2,1,0:T(2,128)(2,1)} %get-tuple-element.16) | data formatting | bytes 1048576 | tf_op jit(solution)/shard_map/reshape;reshape;squeeze | solution.py:22
  56.4 2.2 %fusion.134 = (f32[32,8]{1,0:T(8,128)S(1)}, f32[32,8,1024]{2,1,0:T(8,128)}) fusion(bf16[1024,8,128]{0,2,1:T(8,128)(2,1)S(1)} %bitcast.460, bf16[32,8,8,128]{3,2,1,0:T(8,128)(2,1)} %reshape_reshape_squeeze.7), kind=kOutput, calls=%fused_computation.258 | convolution fusion | flops 67632896 | bytes 1377280 | tf_op jit(solution)/shard_map/rgd,td->rgt/dot_general | solution.py:29
  58.6 2.7 %fusion.135 = (f32[32,8]{1,0:T(8,128)}, f32[32,8,1024]{2,1,0:T(8,128)}) fusion(bf16[1024,8,128]{0,2,1:T(8,128)(2,1)S(1)} %bitcast.461, bf16[32,8,8,128]{3,2,1,0:T(8,128)(2,1)} %reshape_reshape_squeeze.7), kind=kOutput, calls=%fused_computation.259 | convolution fusion | flops 67632896 | bytes 1377280 | tf_op jit(solution)/shard_map/rgd,td->rgt/dot_general | solution.py:29
  61.3 1.3 fusion.136
  63.9 1.4 %fusion.138 = (f32[32,8]{1,0:T(8,128)S(1)}, f32[32,8,1024]{2,1,0:T(8,128)}) fusion(bf16[1024,8,128]{0,2,1:T(8,128)(2,1)S(1)} %bitcast.464, bf16[32,8,8,128]{3,2,1,0:T(8,128)(2,1)S(1)} %copy-done.19), kind=kOutput, calls=%fused_computation.262 | convolution fusion | flops 67632896 | bytes 1377280 | tf_op jit(solution)/shard_map/rgd,td->rgt/dot_general | solution.py:29
  76.3 2.0 %stack_reshape_reshape.14 = bf16[16,1,2,8192]{3,2,0,1:T(2,128)(2,1)} reshape(bf16[32,8,8,128]{3,2,1,0:T(8,128)(2,1)} %copy.301) | data formatting | bytes 1048576 | tf_op jit(solution)/shard_map/stack;reshape;reshape | solution.py:63
  79.6 1.6 %fusion.31 = bf16[32,8,8,128]{3,2,0,1:T(8,128)(2,1)S(1)} fusion(f32[32,8,1024]{2,1,0:T(8,128)S(1)} %copy-done.9, f32[32,8]{1,0:T(8,128)} %copy-done.36, bf16[1024,8,128]{0,2,1:T(8,128)(2,1)} %bitcast.477, f32[32,8]{1,0:T(8,128)S(1)} %fusion.69), kind=kOutput, calls=%fused_computation.68 | convolution fusion | flops 67698688 | bytes 1393664 | tf_op jit(solution)/shard_map/rgt,td->rgd/dot_general | solution.py:42
  88.5 6.9 %all-to-all-start.1 = ((f32[16,1,256]{2,1,0:T(1,128)}), f32[16,1,256]{2,1,0:T(1,128)S(1)}, u32[]{:S(2)}, u32[]{:S(2)}) async-start(f32[16,1,256]{2,1,0:T(1,128)} %reshape.539), calls=%async_computation.1 | async-start | bytes 32768 | tf_op jit(solution)/shard_map/all_to_all | solution.py:152
  95.4 1.5 %pad_maximum_fusion = bf16[16,2,2,8192]{3,2,0,1:T(2,128)(2,1)S(1)} fusion(bf16[16,1,2,8192]{3,2,0,1:T(2,128)(2,1)S(1)} %stack_reshape_reshape.15, bf16[16,1,2,8192]{3,2,0,1:T(2,128)(2,1)S(1)} %copy-done.22), kind=kLoop, calls=%fused_computation.89 | loop fusion | flops 524288 | bytes 2097152 | tf_op jit(solution)/shard_map/stack | solution.py:63
  96.9 1.9 %copy.312 = bf16[16,2,2,8192]{3,2,1,0:T(2,128)(2,1)} copy(bf16[16,2,2,8192]{3,2,0,1:T(2,128)(2,1)S(1)} %pad_maximum_fusion) | data formatting | bytes 2097152 | tf_op jit(solution)/shard_map/stack | solution.py:63
  98.8 3.1 %all-to-all-done.1 = f32[16,1,256]{2,1,0:T(1,128)S(1)} async-done(((f32[16,1,256]{2,1,0:T(1,128)}), f32[16,1,256]{2,1,0:T(1,128)S(1)}, u32[]{:S(2)}, u32[]{:S(2)}) %all-to-all-start.1) | async-done | bytes 16416 | tf_op jit(solution)/shard_map/all_to_all | solution.py:152
  101.9 3.7 %all-to-all-start.2 = ((bf16[16,2,2,8192]{3,2,1,0:T(2,128)(2,1)}), bf16[16,2,2,8192]{3,2,1,0:T(2,128)(2,1)S(1)}, u32[]{:S(2)}, u32[]{:S(2)}) async-start(bf16[16,2,2,8192]{3,2,1,0:T(2,128)(2,1)} %copy.312), calls=%async_computation.2 | async-start | bytes 2097152 | tf_op jit(solution)/shard_map/all_to_all | solution.py:151
  105.7 2.0 %select_reduce_fusion = (f32[16,8,8]{2,1,0:T(8,128)S(1)}, f32[16,8,8,32]{3,2,1,0:T(8,128)S(1)}) fusion(pred[16,32]{1,0:T(8,128)(4,1)S(1)} %iota_compare_fusion.2, bf16[16,8,8,128]{3,2,1,0:T(8,128)(2,1)S(1)} %bitcast.498, bf16[16,32,1024]{2,1,0:T(8,128)(2,1)} %param.14), kind=kOutput, calls=%fused_computation.144 | convolution fusion | flops 8485888 | bytes 1446400 | tf_op jit(solution)/shard_map/rhgd,rthd->rhgt/dot_general | solution.py:75
  111.7 16.8 %all-to-all-done.2 = bf16[16,2,2,8192]{3,2,1,0:T(2,128)(2,1)S(1)} async-done(((bf16[16,2,2,8192]{3,2,1,0:T(2,128)(2,1)}), bf16[16,2,2,8192]{3,2,1,0:T(2,128)(2,1)S(1)}, u32[]{:S(2)}, u32[]{:S(2)}) %all-to-all-start.2) | async-done | bytes 1048608 | tf_op jit(solution)/shard_map/all_to_all | solution.py:151
  130.8 1.8 %fusion.100 = bf16[16,8192]{1,0:T(8,128)(2,1)} fusion(f32[2,8,64,128]{3,2,1,0:T(8,128)S(1)} %bitcast.496, f32[2,8,64,128]{3,2,1,0:T(8,128)S(1)} %bitcast.500, f32[2,8,64,128]{3,2,1,0:T(8,128)S(1)} %bitcast.495, f32[2,8,64,128]{3,2,1,0:T(8,128)S(1)} %bitcast.494), kind=kLoop, calls=%fused_computation.140 | loop fusion | flops 524288 | bytes 2359296 | tf_op jit(solution)/shard_map/convert_element_type | solution.py:106
  (204 shorter events, 34.6 us)
Async XLA Ops:
  0.0 108.2 %copy-start = (bf16[16,32,1024]{2,1,0:T(8,128)(2,1)S(1)}, bf16[16,32,1024]{2,1,0:T(8,128)(2,1)}, u32[]{:S(2)}) copy-start(bf16[16,32,1024]{2,1,0:T(8,128)(2,1)} %param.15) | copy-start | bytes 3145732
  5.5 30.4 %all-to-all-start = ((bf16[16,2,2,8192]{3,2,1,0:T(2,128)(2,1)}), bf16[16,2,2,8192]{3,2,1,0:T(2,128)(2,1)}, u32[]{:S(2)}, u32[]{:S(2)}) async-start(bf16[16,2,2,8192]{3,2,1,0:T(2,128)(2,1)} %reshape.484), calls=%async_computation | async-start | bytes 2097152 | tf_op jit(solution)/shard_map/all_to_all | solution.py:147
  29.1 5.3 %copy-start.23 = (bf16[16,8192]{1,0:T(8,128)(2,1)S(1)}, bf16[16,8192]{1,0:T(8,128)(2,1)}, u32[]{:S(2)}) copy-start(bf16[16,8192]{1,0:T(8,128)(2,1)} %param.8) | copy-start | bytes 786436
  41.6 4.7 %copy-start.1 = (bf16[1,1024,1024]{1,2,0:T(8,128)(2,1)S(1)}, bf16[1,1024,1024]{1,2,0:T(8,128)(2,1)}, u32[]{:S(2)}) copy-start(bf16[1,1024,1024]{1,2,0:T(8,128)(2,1)} %copy.316) | copy-start | bytes 6291460
  41.6 4.7 %copy-start.18 = (bf16[32,8,8,128]{3,2,1,0:T(8,128)(2,1)S(1)}, bf16[32,8,8,128]{3,2,1,0:T(8,128)(2,1)}, u32[]{:S(2)}) copy-start(bf16[32,8,8,128]{3,2,1,0:T(8,128)(2,1)} %reshape_reshape_squeeze.6) | copy-start | bytes 1572868
  46.4 23.7 %copy-start.34 = (f32[32,8]{1,0:T(8,128)}, f32[32,8]{1,0:T(8,128)S(1)}, u32[]{:S(2)}) copy-start(f32[32,8]{1,0:T(8,128)S(1)} %get-tuple-element.35) | copy-start | bytes 3076
  47.7 23.2 %copy-start.32 = (f32[32,8]{1,0:T(8,128)}, f32[32,8]{1,0:T(8,128)S(1)}, u32[]{:S(2)}) copy-start(f32[32,8]{1,0:T(8,128)S(1)} %get-tuple-element.37) | copy-start | bytes 3076
  49.0 22.7 %copy-start.30 = (f32[32,8]{1,0:T(8,128)}, f32[32,8]{1,0:T(8,128)S(1)}, u32[]{:S(2)}) copy-start(f32[32,8]{1,0:T(8,128)S(1)} %get-tuple-element.39) | copy-start | bytes 3076
  50.3 22.2 %copy-start.26 = (f32[32,8]{1,0:T(8,128)}, f32[32,8]{1,0:T(8,128)S(1)}, u32[]{:S(2)}) copy-start(f32[32,8]{1,0:T(8,128)S(1)} %get-tuple-element.41) | copy-start | bytes 3076
  56.4 4.9 %copy-start.19 = (bf16[32,8,8,128]{3,2,1,0:T(8,128)(2,1)S(1)}, bf16[32,8,8,128]{3,2,1,0:T(8,128)(2,1)}, u32[]{:S(2)}) copy-start(bf16[32,8,8,128]{3,2,1,0:T(8,128)(2,1)} %reshape_reshape_squeeze.7) | copy-start | bytes 1572868
  58.6 19.8 %copy-start.36 = (f32[32,8]{1,0:T(8,128)}, f32[32,8]{1,0:T(8,128)S(1)}, u32[]{:S(2)}) copy-start(f32[32,8]{1,0:T(8,128)S(1)} %get-tuple-element.17) | copy-start | bytes 3076
  65.2 3.8 %copy-start.17 = (f32[32,8,1024]{2,1,0:T(8,128)S(1)}, f32[32,8,1024]{2,1,0:T(8,128)}, u32[]{:S(2)}) copy-start(f32[32,8,1024]{2,1,0:T(8,128)} %get-tuple-element.34) | copy-start | bytes 3145732
  66.5 2.9 %copy-start.21 = (bf16[1,1024,1024]{1,2,0:T(8,128)(2,1)S(1)}, bf16[1,1024,1024]{1,2,0:T(8,128)(2,1)}, u32[]{:S(2)}) copy-start(bf16[1,1024,1024]{1,2,0:T(8,128)(2,1)} %copy.349) | copy-start | bytes 6291460
  67.8 2.0 %copy-start.16 = (f32[32,8,1024]{2,1,0:T(8,128)S(1)}, f32[32,8,1024]{2,1,0:T(8,128)}, u32[]{:S(2)}) copy-start(f32[32,8,1024]{2,1,0:T(8,128)} %get-tuple-element.36) | copy-start | bytes 3145732
  73.3 1.3 copy-start.10
  74.9 3.4 %copy-start.49 = (f32[32,8]{1,0:T(8,128)}, f32[32,8]{1,0:T(8,128)S(1)}, u32[]{:S(2)}) copy-start(f32[32,8]{1,0:T(8,128)S(1)} %fusion.67) | copy-start | bytes 3076
  74.9 3.4 %copy-start.9 = (f32[32,8,1024]{2,1,0:T(8,128)S(1)}, f32[32,8,1024]{2,1,0:T(8,128)}, u32[]{:S(2)}) copy-start(f32[32,8,1024]{2,1,0:T(8,128)} %get-tuple-element.18) | copy-start | bytes 3145732
  76.3 4.9 %copy-start.8 = (f32[32,8,1024]{2,1,0:T(8,128)S(1)}, f32[32,8,1024]{2,1,0:T(8,128)}, u32[]{:S(2)}) copy-start(f32[32,8,1024]{2,1,0:T(8,128)} %get-tuple-element.20) | copy-start | bytes 3145732
  78.3 2.8 %copy-start.28 = (f32[32,8]{1,0:T(8,128)S(1)}, f32[32,8]{1,0:T(8,128)}, u32[]{:S(2)}) copy-start(f32[32,8]{1,0:T(8,128)} %get-tuple-element.19) | copy-start | bytes 3076
  78.3 3.1 %copy-start.20 = (bf16[1,1024,1024]{1,2,0:T(8,128)(2,1)S(1)}, bf16[1,1024,1024]{1,2,0:T(8,128)(2,1)}, u32[]{:S(2)}) copy-start(bf16[1,1024,1024]{1,2,0:T(8,128)(2,1)} %copy.358) | copy-start | bytes 6291460
  79.6 2.3 %copy-start.7 = (f32[32,8,1024]{2,1,0:T(8,128)S(1)}, f32[32,8,1024]{2,1,0:T(8,128)}, u32[]{:S(2)}) copy-start(f32[32,8,1024]{2,1,0:T(8,128)} %get-tuple-element.22) | copy-start | bytes 3145732
  82.2 1.3 copy-start.5
  83.0 1.3 copy-start.4
  83.8 1.3 copy-start.3
  84.6 1.3 copy-start.2
  86.7 8.7 %copy-start.22 = (bf16[16,1,2,8192]{3,2,0,1:T(2,128)(2,1)S(1)}, bf16[16,1,2,8192]{3,2,0,1:T(2,128)(2,1)}, u32[]{:S(2)}) copy-start(bf16[16,1,2,8192]{3,2,0,1:T(2,128)(2,1)} %stack_reshape_reshape.14) | copy-start | bytes 1572868
  88.5 13.4 %all-to-all-start.1 = ((f32[16,1,256]{2,1,0:T(1,128)}), f32[16,1,256]{2,1,0:T(1,128)S(1)}, u32[]{:S(2)}, u32[]{:S(2)}) async-start(f32[16,1,256]{2,1,0:T(1,128)} %reshape.539), calls=%async_computation.1 | async-start | bytes 32768 | tf_op jit(solution)/shard_map/all_to_all | solution.py:152
  96.9 8.7 %copy-start.52 = (s32[16]{0:T(128)S(1)}, s32[16]{0:T(128)}, u32[]{:S(2)}) copy-start(s32[16]{0:T(128)} %param.10) | copy-start | bytes 196
  96.9 8.7 %copy-start.24 = (bf16[2,8,64,128]{3,2,1,0:T(8,128)(2,1)S(1)}, bf16[2,8,64,128]{3,2,1,0:T(8,128)(2,1)}, u32[]{:S(2)}) copy-start(bf16[2,8,64,128]{3,2,1,0:T(8,128)(2,1)} %copy.369) | copy-start | bytes 786436
  98.8 9.4 %copy-start.53 = (s32[32,1]{0,1:T(1,128)S(1)}, s32[32,1]{0,1:T(1,128)}, u32[]{:S(2)}) copy-start(s32[32,1]{0,1:T(1,128)} %add.345) | copy-start | bytes 388
  101.9 26.6 %all-to-all-start.2 = ((bf16[16,2,2,8192]{3,2,1,0:T(2,128)(2,1)}), bf16[16,2,2,8192]{3,2,1,0:T(2,128)(2,1)S(1)}, u32[]{:S(2)}, u32[]{:S(2)}) async-start(bf16[16,2,2,8192]{3,2,1,0:T(2,128)(2,1)} %copy.312), calls=%async_computation.2 | async-start | bytes 2097152 | tf_op jit(solution)/shard_map/all_to_all | solution.py:151
  108.1 3.3 %copy-start.51 = (pred[16,2]{1,0:T(8,128)(4,1)S(1)}, pred[16,2]{1,0:T(8,128)(4,1)}, u32[]{:S(2)}) copy-start(pred[16,2]{1,0:T(8,128)(4,1)} %copy.249) | copy-start | bytes 100
  (25 other events, 26.3 us)
where the time goes:
time: 135 us; the launch traced here: 133 us
  local copies, waits for them, and re-layouts  42.3 us (31%)
  matrix products  37 us (27%)
  waiting for transfers between devices  20.7 us (15%)
  starting transfers between devices  18 us (13%)
  other arithmetic  13.6 us (10%)
    dot_general x16, matrix products, span_terms(): jnp.einsum('rgd,td->rgt', query_heads[:, kv_head], key_heads[:, kv_head],...  25.1 us
    all_to_all x1, waiting for transfers between devices, body(): lax.all_to_all(part_out, 'owner', split_axis=0, concat_axis=0, tiled=True)  16.8 us
    unnamed x116, local copies, waits for them, and re-layouts  15.1 us
    all_to_all x1, starting transfers between devices, body(): lax.all_to_all(outgoing, 'owner', split_axis=0, concat_axis=0, tiled=True)  7.44 us
    dot_general x16, matrix products, span_terms(): jnp.einsum('rgt,td->rgd', weights, value_heads[:, kv_head], preferred_ele...  7.25 us
    all_to_all x1, starting transfers between devices, body(): lax.all_to_all(part_lse, 'owner', split_axis=0, concat_axis=0, tiled=True)  6.88 us
    reduce_sum x16, other arithmetic, span_terms(): summed = jnp.sum(expon, axis=-1)  4.77 us
    another operation x2, local copies, waits for them, and re-layouts, span_terms(): query_heads = rows.reshape(row_count, KV_HEADS, per_group, HEAD_DIM)  4.47 us
  transfers between devices with their start and end apart: 3, of which 3 were waited for; matrix products, arithmetic and copies ran while one was open for 24% of the time, Pallas kernels for 0%

commit v1 on v0

v1 whole, which is shorter than its diff:
```python
import functools
import math

import jax
import jax.numpy as jnp
from jax import lax
from jax.experimental import pallas as pl
from jax.experimental.pallas import tpu as pltpu
from jax.sharding import PartitionSpec as P

HEADS = 64
KV_HEADS = 8
HEAD_DIM = 128
PREFIXES = 16
CAP = 2
GROUP = HEADS // KV_HEADS
PAIR = 2
FACTOR = 1.0 / math.sqrt(HEAD_DIM)
LOG2E = math.log2(math.e)
NEG_FILL = -1e30
VMEM_LIMIT = 48 * 1024 * 1024


def row_positions(prefix_ref, map_ref, count_ref, rows, per_prefix, visit):
    for p in range(PREFIXES):
        count_ref[p] = 0
    for r in range(rows):
        p = prefix_ref[r]
        rank = count_ref[p]
        count_ref[p] = rank + 1
        for c in range(per_prefix):
            visit(r, c, map_ref[p * per_prefix + c] * CAP + rank)


def dispatch_kernel(prefix_ref, map_ref, q_ref, out_ref, count_ref):
    out_ref[...] = jnp.zeros_like(out_ref)

    def visit(r, c, pos):
        out_ref[pos] = q_ref[r]

    row_positions(
        prefix_ref, map_ref, count_ref, q_ref.shape[0], map_ref.shape[0] // PREFIXES, visit
    )


def span_kernel(q_ref, k_ref, v_ref, out_ref, lse_ref, *, sources, slots, chunk):
    step = pl.program_id(0)

    @pl.when(step == 0)
    def _():
        lse_ref[...] = jnp.zeros_like(lse_ref)

    heads = PAIR * GROUP
    per = chunk * CAP
    for first in range(0, sources, chunk):
        for slot in range(slots):
            q = q_ref[pl.ds(first, chunk), slot].astype(jnp.float32).reshape(per, heads, HEAD_DIM)
            outs = []
            lses = []
            for j in range(PAIR):
                cols = slice(j * HEAD_DIM, (j + 1) * HEAD_DIM)
                qj = q[:, j * GROUP : (j + 1) * GROUP].reshape(per * GROUP, HEAD_DIM)
                raw = lax.dot_general(
                    qj.astype(jnp.bfloat16),
                    k_ref[slot, :, cols],
                    (((1,), (1,)), ((), ())),
                    preferred_element_type=jnp.float32,
                )
                highest = jnp.max(raw, axis=-1, keepdims=True)
                expon = jnp.exp2((raw - highest) * (FACTOR * LOG2E))
                total = jnp.sum(expon, axis=-1, keepdims=True)
                mixed = jnp.dot(
                    expon.astype(jnp.bfloat16),
                    v_ref[slot, :, cols],
                    preferred_element_type=jnp.float32,
                )
                outs.append((mixed / total).reshape(per, GROUP, HEAD_DIM))
                lse = highest * FACTOR + jnp.log(total)
                lses.append(
                    jnp.broadcast_to(lse, (per * GROUP, HEAD_DIM)).reshape(per, GROUP, HEAD_DIM)
                )
            shape = (per, heads, HEAD_DIM)
            out_ref[pl.ds(first, chunk), slot] = (
                jnp.concatenate(outs, axis=1)
                .astype(jnp.bfloat16)
                .reshape(chunk, CAP, heads, HEAD_DIM)
            )
            own = lax.broadcasted_iota(jnp.int32, shape, 2) == (
                lax.broadcasted_iota(jnp.int32, shape, 1) + step * heads
            )
            placed = jnp.sum(jnp.where(own, jnp.concatenate(lses, axis=1), 0.0), axis=1)
            lse_ref[slot, pl.ds(first * CAP, per)] += placed


def finish_kernel(
    prefix_ref,
    map_ref,
    len_ref,
    q_ref,
    sk_ref,
    sv_ref,
    back_ref,
    lse_ref,
    out_ref,
    count_ref,
    sel_ref,
    sel_lse_ref,
):
    step = pl.program_id(0)
    rows = q_ref.shape[0]
    per_prefix = map_ref.shape[0] // PREFIXES
    heads = PAIR * GROUP
    tokens = sk_ref.shape[0]
    room = tokens // rows

    def visit(r, c, pos):
        sel_ref[c, r] = back_ref[pos]
        sel_lse_ref[c, pl.ds(r, 1)] = lse_ref[pl.ds(pos, 1)]

    row_positions(prefix_ref, map_ref, count_ref, rows, per_prefix, visit)

    col = lax.broadcasted_iota(jnp.int32, (1, tokens), 1)
    limit = jnp.zeros((1, tokens), jnp.int32)
    for r in range(rows):
        limit = jnp.where(col // room == r, r * room + len_ref[r], limit)
    owner_row = lax.broadcasted_iota(jnp.int32, (rows * GROUP, tokens), 0) // GROUP
    visible = (owner_row == col // room) & (col < limit)
    q = q_ref[...].astype(jnp.float32)
    results = []
    lane = lax.broadcasted_iota(jnp.int32, (rows, GROUP, HEAD_DIM), 2)
    within = lax.broadcasted_iota(jnp.int32, (rows, GROUP, HEAD_DIM), 1)
    for j in range(PAIR):
        cols = slice(j * HEAD_DIM, (j + 1) * HEAD_DIM)
        part = slice(j * GROUP, (j + 1) * GROUP)
        qj = q[:, part].reshape(rows * GROUP, HEAD_DIM).astype(jnp.bfloat16)
        raw = lax.dot_general(
            qj, sk_ref[:, cols], (((1,), (1,)), ((), ())), preferred_element_type=jnp.float32
        )
        raw = jnp.where(visible, raw, NEG_FILL)
        highest = jnp.max(raw, axis=-1, keepdims=True)
        expon = jnp.where(visible, jnp.exp2((raw - highest) * (FACTOR * LOG2E)), 0.0)
        total = jnp.sum(expon, axis=-1, keepdims=True)
        mixed = jnp.dot(
            expon.astype(jnp.bfloat16), sv_ref[:, cols], preferred_element_type=jnp.float32
        )
        suffix_out = (mixed / total).reshape(rows, GROUP, HEAD_DIM)
        suffix_lse = (highest * FACTOR + jnp.log(total)).reshape(rows, GROUP, 1)
        mine = lane == within + (step * heads + j * GROUP)
        span_lse = []
        top = suffix_lse
        for c in range(per_prefix):
            wide = jnp.broadcast_to(sel_lse_ref[c][:, None, :], (rows, GROUP, HEAD_DIM))
            one = jnp.sum(jnp.where(mine, wide, 0.0), axis=-1, keepdims=True)
            span_lse.append(one)
            top = jnp.maximum(top, one)
        scale = jnp.exp(suffix_lse - top)
        numerator = scale * suffix_out
        denominator = scale
        for c in range(per_prefix):
            scale = jnp.exp(span_lse[c] - top)
            numerator += scale * sel_ref[c].astype(jnp.float32)[:, part]
            denominator += scale
        results.append(numerator / denominator)
    out_ref[...] = jnp.concatenate(results, axis=1).astype(jnp.bfloat16)


def body(
    queries,
    request_prefix,
    suffix_len,
    block_map,
    prefix_keys,
    prefix_values,
    suffix_keys,
    suffix_values,
):
    owners = lax.axis_size("owner")
    rows = queries.shape[0]
    slot_count = block_map.shape[0]
    slots, span, width = prefix_keys.shape
    per_prefix = slot_count // PREFIXES
    buffer = slot_count * CAP
    heads = PAIR * GROUP
    steps = HEADS // heads
    cols = PAIR * HEAD_DIM
    params = pltpu.CompilerParams(vmem_limit_bytes=VMEM_LIMIT)
    smem = pl.BlockSpec(memory_space=pltpu.SMEM)
    vmem = pl.BlockSpec(memory_space=pltpu.VMEM)
    prefix_ids = request_prefix.reshape(rows)
    q3 = queries.reshape(rows, HEADS, HEAD_DIM)

    outgoing = pl.pallas_call(
        dispatch_kernel,
        out_shape=jax.ShapeDtypeStruct((buffer, HEADS, HEAD_DIM), jnp.bfloat16),
        in_specs=[smem, smem, vmem],
        out_specs=vmem,
        scratch_shapes=[pltpu.SMEM((PREFIXES,), jnp.int32)],
        compiler_params=params,
        name="dispatch",
    )(prefix_ids, block_map, q3)
    received = lax.all_to_all(outgoing, "owner", split_axis=0, concat_axis=0, tiled=True)

    chunk = math.gcd(owners, 16)
    block = (owners, slots, CAP, heads, HEAD_DIM)
    row_spec = pl.BlockSpec(block, lambda i: (0, 0, 0, i, 0))
    kv_spec = pl.BlockSpec((slots, span, cols), lambda i: (0, 0, i))
    part_out, part_lse = pl.pallas_call(
        functools.partial(span_kernel, sources=owners, slots=slots, chunk=chunk),
        grid=(steps,),
        out_shape=(
            jax.ShapeDtypeStruct((owners, slots, CAP, HEADS, HEAD_DIM), jnp.bfloat16),
            jax.ShapeDtypeStruct((slots, owners * CAP, HEAD_DIM), jnp.float32),
        ),
        in_specs=[row_spec, kv_spec, kv_spec],
        out_specs=(
            row_spec,
            pl.BlockSpec((slots, owners * CAP, HEAD_DIM), lambda i: (0, 0, 0)),
        ),
        compiler_params=params,
        name="span_attention",
    )(received.reshape(owners, slots, CAP, HEADS, HEAD_DIM), prefix_keys, prefix_values)
    part_lse = (
        part_lse.reshape(slots, owners, CAP, HEAD_DIM)
        .transpose(1, 0, 2, 3)
        .reshape(owners, slots * CAP, HEAD_DIM)
    )
    back_lse = lax.all_to_all(part_lse, "owner", split_axis=0, concat_axis=0, tiled=True)
    back_out = lax.all_to_all(
        part_out.reshape(buffer, HEADS, HEAD_DIM), "owner", split_axis=0, concat_axis=0, tiled=True
    )

    tokens = rows * suffix_keys.shape[1]
    head_rows = pl.BlockSpec((rows, heads, HEAD_DIM), lambda i: (0, i, 0))
    suffix_spec = pl.BlockSpec((tokens, cols), lambda i: (0, i))
    out = pl.pallas_call(
        finish_kernel,
        grid=(steps,),
        out_shape=jax.ShapeDtypeStruct((rows, HEADS, HEAD_DIM), jnp.bfloat16),
        in_specs=[
            smem,
            smem,
            smem,
            head_rows,
            suffix_spec,
            suffix_spec,
            pl.BlockSpec((buffer, heads, HEAD_DIM), lambda i: (0, i, 0)),
            pl.BlockSpec((buffer, HEAD_DIM), lambda i: (0, 0)),
        ],
        out_specs=head_rows,
        scratch_shapes=[
            pltpu.SMEM((PREFIXES,), jnp.int32),
            pltpu.VMEM((per_prefix, rows, heads, HEAD_DIM), jnp.bfloat16),
            pltpu.VMEM((per_prefix, rows, HEAD_DIM), jnp.float32),
        ],
        compiler_params=params,
        name="suffix_combine",
    )(
        prefix_ids,
        block_map,
        suffix_len,
        q3,
        suffix_keys.reshape(tokens, width),
        suffix_values.reshape(tokens, width),
        back_out,
        back_lse.reshape(buffer, HEAD_DIM),
    )
    return out.reshape(rows, HEADS * HEAD_DIM)


def solution(mesh):
    placed = (
        P(("groups", "owner"), None),
        P(("groups", "owner"), None),
        P(("groups", "owner")),
        P("groups"),
        P(("groups", "owner"), None, None),
        P(("groups", "owner"), None, None),
        P(("groups", "owner"), None, None),
        P(("groups", "owner"), None, None),
    )
    return jax.shard_map(
        body, mesh=mesh, in_specs=placed, out_specs=P(("groups", "owner"), None), check_vma=False
    )
```

time: 135 us -> 90 us (0.67); the launches traced: 133 us -> 89.5 us
  blocking collectives: 0 us -> 70.9 us
  local copies, waits for them, and re-layouts: 42.3 us -> 3.21 us
  matrix products: 37 us -> 0 us
  waiting for transfers between devices: 20.7 us -> 0 us
  starting transfers between devices: 18 us -> 0 us
  Pallas kernels: 0 us -> 15.3 us
  other arithmetic: 13.6 us -> 0 us
    all_to_all x0 -> x3, blocking collectives: none -> 70.9 us  [the longest x1 32 us: body(): lax.all_to_all(outgoing, 'owner', split_axis=0, concat_axis=0, tiled=True)]
    dot_general x35 -> x0, matrix products: 37 us -> none  [the longest x16 25.1 us: span_terms(): jnp.einsum('rgd,td->rgt', query_heads[:, kv_head], key_heads[:, kv_head],...]
    all_to_all x3 -> x0, waiting for transfers between devices: 20.7 us -> none  [the longest x1 16.8 us: body(): lax.all_to_all(part_out, 'owner', split_axis=0, concat_axis=0, tiled=True)]
    all_to_all x3 -> x0, starting transfers between devices: 18 us -> none  [the longest x1 7.44 us: body(): lax.all_to_all(outgoing, 'owner', split_axis=0, concat_axis=0, tiled=True)]
    pallas_call x0 -> x3, Pallas kernels: none -> 15.3 us  [the longest x1 10.6 us: body(): pl.pallas_call(functools.partial(span_kernel, sources=owners, slots=slots...]
    unnamed x116 -> x16, local copies, waits for them, and re-layouts: 15.1 us -> 3.19 us
    slice x3 -> x0, local copies, waits for them, and re-layouts: 11.5 us -> none  [the longest x1 4.01 us: attend_rows(): prefix_keys[slot_index]]
    another operation x12 -> x0, local copies, waits for them, and re-layouts: 9.97 us -> none  [the longest x2 4.47 us: span_terms(): query_heads = rows.reshape(row_count, KV_HEADS, per_group, HEAD_DIM)]
  transfers between devices with their start and end apart: 3 -> 0, of which waited for: 3 -> 0; matrix products, arithmetic and copies ran while one was open for 24% -> 0% of each run, Pallas kernels for 0% -> 0%
where the time goes in v1:
time: 90 us; the launch traced here: 89.5 us
  blocking collectives  70.9 us (79%)
  Pallas kernels  15.3 us (17%)
  local copies, waits for them, and re-layouts  3.21 us (4%)
    all_to_all x1, blocking collectives, body(): lax.all_to_all(outgoing, 'owner', split_axis=0, concat_axis=0, tiled=True)  32 us
    all_to_all x1, blocking collectives, body(): lax.all_to_all(part_out.reshape(buffer, HEADS, HEAD_DIM), 'owner', split_...  27.4 us
    all_to_all x1, blocking collectives, body(): lax.all_to_all(part_lse, 'owner', split_axis=0, concat_axis=0, tiled=True)  11.4 us
    pallas_call x1, Pallas kernels, body(): pl.pallas_call(functools.partial(span_kernel, sources=owners, slots=slots...  10.6 us
    pallas_call x1, Pallas kernels, body(): pl.pallas_call(finish_kernel, grid=(steps,), out_shape=jax.ShapeDtypeStru...  3.97 us
    unnamed x16, local copies, waits for them, and re-layouts  3.19 us

profile of v1, /device:TPU:0, one launch (start us, length us, event | category | flops | bytes accessed | tf_op | source)
XLA Modules:
  0.0 89.5 jit_solution(5488236364694060013)
XLA Ops:
  0.0 1.0 %copy.10 = bf16[2,8,64,128]{3,2,1,0:T(8,128)(2,1)S(1)} copy(bf16[2,8,64,128]{3,1,2,0:T(8,128)(2,1)} %bitcast.27) | data formatting | bytes 524288
  1.0 0.0 copy-start.2
  1.0 0.6 copy-done.2
  1.7 0.0 copy-start.4
  1.7 0.7 copy-done.4
  2.3 0.8 dispatch.1
  3.1 32.0 %all_to_all.15 = bf16[64,64,128]{2,1,0:T(8,128)(2,1)S(1)} all-to-all(bf16[64,64,128]{2,1,0:T(8,128)(2,1)S(1)} %dispatch.1), channel_id=1, replica_groups=mesh['groups'=2,'owner'=16] {'owner'}, dimensions={0} | all-to-all | bytes 2097152 | tf_op jit(solution)/shard_map/all_to_all | solution.py:201
  35.1 0.0 copy-start
  35.1 0.0 copy-start.1
  35.1 0.0 copy-start.3
  35.1 0.0 copy-start.5
  35.1 0.0 copy-start.6
  35.1 10.6 %span_attention.1 = (bf16[16,2,2,64,128]{4,3,2,1,0:T(8,128)(2,1)S(1)}, f32[2,32,128]{2,1,0:T(8,128)S(1)}) custom-call(bf16[16,2,2,64,128]{4,3,2,1,0:T(8,128)(2,1)S(1)} %bitcast.16, bf16[2,1024,1024]{2,1,0:T(8,128)(2,1)} %k_ref.1, bf16[2,1024,1024]{2,1,0:T(8,128)(2,1)} %v_ref.1), custom_call_target="tpu_custom_call" | custom-call | tf_op jit(solution)/shard_map/span_attention/pallas_call | solution.py:207
  45.7 11.4 %all_to_all.16 = f32[16,4,128]{2,1,0:T(4,128)S(1)} all-to-all(f32[16,4,128]{2,1,0:T(4,128)S(1)} %bitcast.28), channel_id=1, replica_groups=mesh['groups'=2,'owner'=16] {'owner'}, dimensions={0} | all-to-all | bytes 65536 | tf_op jit(solution)/shard_map/all_to_all | solution.py:227
  57.2 27.4 %all_to_all.17.back_ref = bf16[64,64,128]{2,1,0:T(8,128)(2,1)S(1)} all-to-all(bf16[64,64,128]{2,1,0:T(8,128)(2,1)S(1)} %bitcast.22), channel_id=1, replica_groups=mesh['groups'=2,'owner'=16] {'owner'}, dimensions={0} | all-to-all | bytes 2097152 | tf_op jit(solution)/shard_map/all_to_all | solution.py:228
  84.6 0.0 copy-done
  84.6 0.0 copy-done.1
  84.6 0.0 copy-done.3
  84.6 0.0 copy-done.5
  84.6 0.0 copy-done.6
  84.6 4.0 %suffix_combine.1 = bf16[16,64,128]{2,1,0:T(8,128)(2,1)S(1)} custom-call(s32[16]{0:T(128)S(1)} %bitcast.26, s32[32]{0:T(128)S(1)} %copy-done.5, s32[16]{0:T(128)S(1)} %copy-done.6, bf16[16,64,128]{2,1,0:T(8,128)(2,1)S(1)} %bitcast.18, bf16[512,1024]{1,0:T(8,128)(2,1)S(1)} %bitcast.19, bf16[512,1024]{1,0:T(8,128)(2,1)S(1)} %bitcast.20, ...), custom_call_target="tpu_custom_call" | custom-call | tf_op jit(solution)/shard_map/suffix_combine/pallas_call | solution.py:235
  88.6 0.9 copy.13
  (1 shorter events, 0.0 us)
Async XLA Ops:
  1.0 0.7 copy-start.2
  1.7 0.7 copy-start.4
  35.1 49.5 %copy-start = (bf16[16,32,1024]{2,1,0:T(8,128)(2,1)S(1)}, bf16[16,32,1024]{2,1,0:T(8,128)(2,1)}, u32[]{:S(2)}) copy-start(bf16[16,32,1024]{2,1,0:T(8,128)(2,1)} %param.14) | copy-start | bytes 3145732
  35.1 49.5 %copy-start.1 = (bf16[16,32,1024]{2,1,0:T(8,128)(2,1)S(1)}, bf16[16,32,1024]{2,1,0:T(8,128)(2,1)}, u32[]{:S(2)}) copy-start(bf16[16,32,1024]{2,1,0:T(8,128)(2,1)} %param.15) | copy-start | bytes 3145732
  35.1 49.5 %copy-start.3 = (s32[16,1]{0,1:T(1,128)S(1)}, s32[16,1]{0,1:T(1,128)}, u32[]{:S(2)}) copy-start(s32[16,1]{0,1:T(1,128)} %param.9) | copy-start | bytes 196
  35.1 49.5 %copy-start.5 = (s32[32]{0:T(128)S(1)}, s32[32]{0:T(128)}, u32[]{:S(2)}) copy-start(s32[32]{0:T(128)} %map_ref.3) | copy-start | bytes 388
  35.1 49.5 %copy-start.6 = (s32[16]{0:T(128)S(1)}, s32[16]{0:T(128)}, u32[]{:S(2)}) copy-start(s32[16]{0:T(128)} %len_ref.1) | copy-start | bytes 196

commit v2 on v1

--- a/solution.py
+++ b/solution.py
@@ -164,6 +164,66 @@
     out_ref[...] = jnp.concatenate(results, axis=1).astype(jnp.bfloat16)
 
 
+def exchange_kernel(*refs, count):
+    sources, targets = refs[:count], refs[count : 2 * count]
+    send_sem, recv_sem, local_sem = refs[2 * count :]
+    me = lax.axis_index("owner")
+    n = lax.axis_size("owner")
+    barrier = pltpu.get_barrier_semaphore()
+    for k in range(1, n):
+        pl.semaphore_signal(
+            barrier,
+            inc=1,
+            device_id={"owner": lax.rem(me + k, n)},
+            device_id_type=pl.DeviceIdType.MESH,
+        )
+    own = [
+        pltpu.make_async_copy(source.at[me], target.at[me], local_sem.at[a])
+        for a, (source, target) in enumerate(zip(sources, targets))
+    ]
+    for copy in own:
+        copy.start()
+    pl.semaphore_wait(barrier, n - 1)
+    copies = []
+    for k in range(1, n):
+        peer = lax.rem(me + k, n)
+        for a, (source, target) in enumerate(zip(sources, targets)):
+            copies.append(
+                pltpu.make_async_remote_copy(
+                    src_ref=source.at[peer],
+                    dst_ref=target.at[me],
+                    send_sem=send_sem.at[a, k],
+                    recv_sem=recv_sem.at[a, k],
+                    device_id={"owner": peer},
+                    device_id_type=pl.DeviceIdType.MESH,
+                )
+            )
+            copies[-1].start()
+    for copy in own + copies:
+        copy.wait()
+
+
+def exchange(arrays, collective_id, name):
+    n = lax.axis_size("owner")
+    count = len(arrays)
+    anywhere = pl.BlockSpec(memory_space=pl.ANY)
+    return pl.pallas_call(
+        functools.partial(exchange_kernel, count=count),
+        out_shape=tuple(jax.ShapeDtypeStruct(a.shape, a.dtype) for a in arrays),
+        in_specs=[anywhere] * count,
+        out_specs=(anywhere,) * count,
+        scratch_shapes=[
+            pltpu.SemaphoreType.DMA((count, n)),
+            pltpu.SemaphoreType.DMA((count, n)),
+            pltpu.SemaphoreType.DMA((count,)),
+        ],
+        compiler_params=pltpu.CompilerParams(
+            collective_id=collective_id, has_side_effects=True, vmem_limit_bytes=VMEM_LIMIT
+        ),
+        name=name,
+    )(*arrays)
+
+
 def body(
     queries,
     request_prefix,
@@ -198,7 +258,9 @@
         compiler_params=params,
         name="dispatch",
     )(prefix_ids, block_map, q3)
-    received = lax.all_to_all(outgoing, "owner", split_axis=0, concat_axis=0, tiled=True)
+    (received,) = exchange(
+        [outgoing.reshape(owners, slots * CAP, HEADS, HEAD_DIM)], 0, "send_queries"
+    )
 
     chunk = math.gcd(owners, 16)
     block = (owners, slots, CAP, heads, HEAD_DIM)
@@ -224,9 +286,8 @@
         .transpose(1, 0, 2, 3)
         .reshape(owners, slots * CAP, HEAD_DIM)
     )
-    back_lse = lax.all_to_all(part_lse, "owner", split_axis=0, concat_axis=0, tiled=True)
-    back_out = lax.all_to_all(
-        part_out.reshape(buffer, HEADS, HEAD_DIM), "owner", split_axis=0, concat_axis=0, tiled=True
+    back_out, back_lse = exchange(
+        [part_out.reshape(owners, slots * CAP, HEADS, HEAD_DIM), part_lse], 1, "send_partials"
     )
 
     tokens = rows * suffix_keys.shape[1]
@@ -261,7 +322,7 @@
         q3,
         suffix_keys.reshape(tokens, width),
         suffix_values.reshape(tokens, width),
-        back_out,
+        back_out.reshape(buffer, HEADS, HEAD_DIM),
         back_lse.reshape(buffer, HEAD_DIM),
     )
     return out.reshape(rows, HEADS * HEAD_DIM)

time: 90 us -> 74.9 us (0.83)
  the two profiles are of different devices: /device:TPU:0 before, /device:TPU:13 now
where the time goes in v2:
time: 74.9 us; the launch traced here: 74.7 us
  Pallas kernels  71.4 us (95%)
  local copies, waits for them, and re-layouts  3.22 us (4%)
    pallas_call x2, Pallas kernels, exchange(): pl.pallas_call(functools.partial(exchange_kernel, count=count), out_shape...  56.1 us
    pallas_call x1, Pallas kernels, body(): pl.pallas_call(functools.partial(span_kernel, sources=owners, slots=slots...  10.6 us
    pallas_call x1, Pallas kernels, body(): pl.pallas_call(finish_kernel, grid=(steps,), out_shape=jax.ShapeDtypeStru...  3.96 us
    unnamed x16, local copies, waits for them, and re-layouts  3.2 us

profile of v2, /device:TPU:13, one launch (start us, length us, event | category | flops | bytes accessed | tf_op | source)
XLA Modules:
  0.0 74.7 jit_solution(14111325848805379310)
XLA Ops:
  0.0 1.0 %copy.10 = bf16[2,8,64,128]{3,2,1,0:T(8,128)(2,1)S(1)} copy(bf16[2,8,64,128]{3,1,2,0:T(8,128)(2,1)} %bitcast.32) | data formatting | bytes 524288
  1.0 0.0 copy-start.2
  1.0 0.6 copy-done.2
  1.7 0.0 copy-start.4
  1.7 0.7 copy-done.4
  2.3 0.8 %dispatch.1 = bf16[64,64,128]{2,1,0:T(8,128)(2,1)S(1)} custom-call(s32[16]{0:T(128)S(1)} %bitcast.30, s32[32]{0:T(128)S(1)} %copy-done.4, bf16[16,64,128]{2,1,0:T(8,128)(2,1)S(1)} %bitcast.20), custom_call_target="tpu_custom_call" | custom-call | tf_op jit(solution)/shard_map/dispatch/pallas_call | solution.py:252
  3.1 28.0 %send_queries.1 = bf16[16,4,64,128]{3,2,1,0:T(8,128)(2,1)S(1)} custom-call(bf16[16,4,64,128]{3,2,1,0:T(8,128)(2,1)S(1)} %bitcast.19), custom_call_target="tpu_custom_call" | custom-call | tf_op jit(solution)/shard_map/send_queries/pallas_call | solution.py:210
  31.1 0.0 copy-start
  31.1 0.0 copy-start.1
  31.1 0.0 copy-start.3
  31.1 0.0 copy-start.5
  31.1 0.0 copy-start.6
  31.1 10.6 %span_attention.1 = (bf16[16,2,2,64,128]{4,3,2,1,0:T(8,128)(2,1)S(1)}, f32[2,32,128]{2,1,0:T(8,128)S(1)}) custom-call(bf16[16,2,2,64,128]{4,3,2,1,0:T(8,128)(2,1)S(1)} %bitcast.18, bf16[2,1024,1024]{2,1,0:T(8,128)(2,1)} %k_ref.1, bf16[2,1024,1024]{2,1,0:T(8,128)(2,1)} %v_ref.1), custom_call_target="tpu_custom_call" | custom-call | tf_op jit(solution)/shard_map/span_attention/pallas_call | solution.py:269
  41.7 28.1 %send_partials.1 = (bf16[16,4,64,128]{3,2,1,0:T(8,128)(2,1)S(1)}, f32[16,4,128]{2,1,0:T(4,128)S(1)}) custom-call(bf16[16,4,64,128]{3,2,1,0:T(8,128)(2,1)S(1)} %bitcast.26, f32[16,4,128]{2,1,0:T(4,128)S(1)} %bitcast.27), custom_call_target="tpu_custom_call" | custom-call | tf_op jit(solution)/shard_map/send_partials/pallas_call | solution.py:210
  69.8 0.0 copy-done
  69.8 0.0 copy-done.1
  69.8 0.0 copy-done.3
  69.8 0.0 copy-done.5
  69.9 0.0 copy-done.6
  69.9 4.0 %suffix_combine.1 = bf16[16,64,128]{2,1,0:T(8,128)(2,1)S(1)} custom-call(s32[16]{0:T(128)S(1)} %bitcast.31, s32[32]{0:T(128)S(1)} %copy-done.5, s32[16]{0:T(128)S(1)} %copy-done.6, bf16[16,64,128]{2,1,0:T(8,128)(2,1)S(1)} %bitcast.21, bf16[512,1024]{1,0:T(8,128)(2,1)S(1)} %bitcast.22, bf16[512,1024]{1,0:T(8,128)(2,1)S(1)} %bitcast.23, ...), custom_call_target="tpu_custom_call" | custom-call | tf_op jit(solution)/shard_map/suffix_combine/pallas_call | solution.py:296
  73.8 0.9 %copy.13 = bf16[2,8,64,128]{3,1,2,0:T(8,128)(2,1)} copy(bf16[2,8,64,128]{3,2,1,0:T(8,128)(2,1)S(1)} %bitcast.25) | data formatting | bytes 524288
  (1 shorter events, 0.0 us)
Async XLA Ops:
  1.0 0.7 copy-start.2
  1.7 0.7 copy-start.4
  31.1 38.8 %copy-start = (bf16[16,32,1024]{2,1,0:T(8,128)(2,1)S(1)}, bf16[16,32,1024]{2,1,0:T(8,128)(2,1)}, u32[]{:S(2)}) copy-start(bf16[16,32,1024]{2,1,0:T(8,128)(2,1)} %param.14) | copy-start | bytes 3145732
  31.1 38.8 %copy-start.1 = (bf16[16,32,1024]{2,1,0:T(8,128)(2,1)S(1)}, bf16[16,32,1024]{2,1,0:T(8,128)(2,1)}, u32[]{:S(2)}) copy-start(bf16[16,32,1024]{2,1,0:T(8,128)(2,1)} %param.15) | copy-start | bytes 3145732
  31.1 38.8 %copy-start.3 = (s32[16,1]{0,1:T(1,128)S(1)}, s32[16,1]{0,1:T(1,128)}, u32[]{:S(2)}) copy-start(s32[16,1]{0,1:T(1,128)} %param.9) | copy-start | bytes 196
  31.1 38.8 %copy-start.5 = (s32[32]{0:T(128)S(1)}, s32[32]{0:T(128)}, u32[]{:S(2)}) copy-start(s32[32]{0:T(128)} %map_ref.3) | copy-start | bytes 388
  31.1 38.8 %copy-start.6 = (s32[16]{0:T(128)S(1)}, s32[16]{0:T(128)}, u32[]{:S(2)}) copy-start(s32[16]{0:T(128)} %len_ref.1) | copy-start | bytes 196

commit v3 on v1

--- a/solution.py
+++ b/solution.py
@@ -43,22 +43,19 @@
     )
 
 
-def span_kernel(q_ref, k_ref, v_ref, out_ref, lse_ref, *, sources, slots, chunk):
-    step = pl.program_id(0)
-
-    @pl.when(step == 0)
-    def _():
-        lse_ref[...] = jnp.zeros_like(lse_ref)
-
+def attend_chunk(step, q_ref, k_ref, v_ref, out_ref, lse_ref, chunk):
+    sources, slots = q_ref.shape[:2]
     heads = PAIR * GROUP
     per = chunk * CAP
+    rows = pl.ds(pl.multiple_of(step * heads, heads), heads)
     for first in range(0, sources, chunk):
         for slot in range(slots):
-            q = q_ref[pl.ds(first, chunk), slot].astype(jnp.float32).reshape(per, heads, HEAD_DIM)
+            q = q_ref[pl.ds(first, chunk), slot, :, rows, :].astype(jnp.float32)
+            q = q.reshape(per, heads, HEAD_DIM)
             outs = []
             lses = []
             for j in range(PAIR):
-                cols = slice(j * HEAD_DIM, (j + 1) * HEAD_DIM)
+                cols = pl.ds(pl.multiple_of((step * PAIR + j) * HEAD_DIM, HEAD_DIM), HEAD_DIM)
                 qj = q[:, j * GROUP : (j + 1) * GROUP].reshape(per * GROUP, HEAD_DIM)
                 raw = lax.dot_general(
                     qj.astype(jnp.bfloat16),
@@ -79,17 +76,143 @@
                 lses.append(
                     jnp.broadcast_to(lse, (per * GROUP, HEAD_DIM)).reshape(per, GROUP, HEAD_DIM)
                 )
-            shape = (per, heads, HEAD_DIM)
-            out_ref[pl.ds(first, chunk), slot] = (
-                jnp.concatenate(outs, axis=1)
-                .astype(jnp.bfloat16)
-                .reshape(chunk, CAP, heads, HEAD_DIM)
+            shape = (chunk, CAP, heads, HEAD_DIM)
+            out_ref[pl.ds(first, chunk), slot, :, rows, :] = (
+                jnp.concatenate(outs, axis=1).astype(jnp.bfloat16).reshape(shape)
             )
-            own = lax.broadcasted_iota(jnp.int32, shape, 2) == (
-                lax.broadcasted_iota(jnp.int32, shape, 1) + step * heads
+            own = lax.broadcasted_iota(jnp.int32, shape, 3) == (
+                lax.broadcasted_iota(jnp.int32, shape, 2) + step * heads
             )
-            placed = jnp.sum(jnp.where(own, jnp.concatenate(lses, axis=1), 0.0), axis=1)
-            lse_ref[slot, pl.ds(first * CAP, per)] += placed
+            lses = jnp.concatenate(lses, axis=1).reshape(shape)
+            lse_ref[pl.ds(first, chunk), slot] += jnp.sum(
+                jnp.where(own, lses, 0.0), axis=2, keepdims=True
+            )
+
+
+def span_kernel(
+    ask_ref,
+    k_hbm,
+    v_hbm,
+    back_ref,
+    back_lse_ref,
+    q_ref,
+    k_ref,
+    v_ref,
+    out_ref,
+    lse_ref,
+    kv_sem,
+    own_sem,
+    ask_send,
+    ask_recv,
+    back_send,
+    back_recv,
+    lse_send,
+    lse_recv,
+    *,
+    chunk,
+):
+    me = lax.axis_index("owner")
+    n = lax.axis_size("owner")
+    heads = PAIR * GROUP
+    steps = HEADS // heads
+
+    def remote(source, target, send_sem, recv_sem, peer):
+        return pltpu.make_async_remote_copy(
+            src_ref=source,
+            dst_ref=target,
+            send_sem=send_sem,
+            recv_sem=recv_sem,
+            device_id={"owner": peer},
+            device_id_type=pl.DeviceIdType.MESH,
+        )
+
+    def peer_of(k):
+        return lax.rem(me + k, n)
+
+    def part(ref, who, step):
+        return ref.at[who, :, :, pl.ds(pl.multiple_of(step * heads, heads), heads), :]
+
+    def ask(step, k):
+        peer = peer_of(k)
+        return remote(
+            part(ask_ref, peer, step),
+            part(q_ref, me, step),
+            ask_send.at[step, k],
+            ask_recv.at[step, k],
+            peer,
+        )
+
+    def answer(step, k):
+        peer = peer_of(k)
+        return remote(
+            part(out_ref, peer, step),
+            part(back_ref, me, step),
+            back_send.at[step, k],
+            back_recv.at[step, k],
+            peer,
+        )
+
+    def answer_lse(k):
+        peer = peer_of(k)
+        return remote(lse_ref.at[peer], back_lse_ref.at[me], lse_send.at[k], lse_recv.at[k], peer)
+
+    def load(step):
+        cols = pl.ds(pl.multiple_of(step * PAIR * HEAD_DIM, HEAD_DIM), PAIR * HEAD_DIM)
+        return [
+            pltpu.make_async_copy(k_hbm.at[:, :, cols], k_ref.at[:, :, cols], kv_sem.at[0, step]),
+            pltpu.make_async_copy(v_hbm.at[:, :, cols], v_ref.at[:, :, cols], kv_sem.at[1, step]),
+        ]
+
+    own_ask = pltpu.make_async_copy(ask_ref.at[me], q_ref.at[me], own_sem.at[0])
+    own_out = pltpu.make_async_copy(out_ref.at[me], back_ref.at[me], own_sem.at[1])
+    own_lse = pltpu.make_async_copy(lse_ref.at[me], back_lse_ref.at[me], own_sem.at[2])
+
+    barrier = pltpu.get_barrier_semaphore()
+    for k in range(1, n):
+        pl.semaphore_signal(
+            barrier,
+            inc=1,
+            device_id={"owner": peer_of(k)},
+            device_id_type=pl.DeviceIdType.MESH,
+        )
+    own_ask.start()
+    lse_ref[...] = jnp.zeros_like(lse_ref)
+    pl.semaphore_wait(barrier, n - 1)
+
+    @pl.loop(0, steps)
+    def _(step):
+        for k in range(1, n):
+            ask(step, k).start()
+        for copy in load(step):
+            copy.start()
+
+    own_ask.wait()
+
+    @pl.loop(0, steps)
+    def _(step):
+        for copy in load(step):
+            copy.wait()
+        for k in range(1, n):
+            ask(step, k).wait_recv()
+        attend_chunk(step, q_ref, k_ref, v_ref, out_ref, lse_ref, chunk)
+        for k in range(1, n):
+            answer(step, k).start()
+
+    own_out.start()
+    own_lse.start()
+    for k in range(1, n):
+        answer_lse(k).start()
+
+    @pl.loop(0, steps)
+    def _(step):
+        for k in range(1, n):
+            ask(step, k).wait_send()
+            answer(step, k).wait()
+
+    for k in range(1, n):
+        answer_lse(k).wait()
+    own_out.wait()
+    own_lse.wait()
 
 
 def finish_kernel(
@@ -115,7 +238,7 @@
 
     def visit(r, c, pos):
         sel_ref[c, r] = back_ref[pos]
-        sel_lse_ref[c, pl.ds(r, 1)] = lse_ref[pl.ds(pos, 1)]
+        sel_lse_ref[c, pl.ds(r, 1)] = lse_ref[pos]
 
     row_positions(prefix_ref, map_ref, count_ref, rows, per_prefix, visit)
 
@@ -177,7 +300,7 @@
     owners = lax.axis_size("owner")
     rows = queries.shape[0]
     slot_count = block_map.shape[0]
-    slots, span, width = prefix_keys.shape
+    slots, _, width = prefix_keys.shape
     per_prefix = slot_count // PREFIXES
     buffer = slot_count * CAP
     heads = PAIR * GROUP
@@ -198,36 +321,38 @@
         compiler_params=params,
         name="dispatch",
     )(prefix_ids, block_map, q3)
-    received = lax.all_to_all(outgoing, "owner", split_axis=0, concat_axis=0, tiled=True)
-
     chunk = math.gcd(owners, 16)
-    block = (owners, slots, CAP, heads, HEAD_DIM)
-    row_spec = pl.BlockSpec(block, lambda i: (0, 0, 0, i, 0))
-    kv_spec = pl.BlockSpec((slots, span, cols), lambda i: (0, 0, i))
-    part_out, part_lse = pl.pallas_call(
-        functools.partial(span_kernel, sources=owners, slots=slots, chunk=chunk),
-        grid=(steps,),
+    items = (owners, slots, CAP, HEADS, HEAD_DIM)
+    lses = (owners, slots, CAP, 1, HEAD_DIM)
+    anywhere = pl.BlockSpec(memory_space=pl.ANY)
+    back_out, back_lse = pl.pallas_call(
+        functools.partial(span_kernel, chunk=chunk),
         out_shape=(
-            jax.ShapeDtypeStruct((owners, slots, CAP, HEADS, HEAD_DIM), jnp.bfloat16),
-            jax.ShapeDtypeStruct((slots, owners * CAP, HEAD_DIM), jnp.float32),
+            jax.ShapeDtypeStruct(items, jnp.bfloat16),
+            jax.ShapeDtypeStruct(lses, jnp.float32),
         ),
-        in_specs=[row_spec, kv_spec, kv_spec],
-        out_specs=(
-            row_spec,
-            pl.BlockSpec((slots, owners * CAP, HEAD_DIM), lambda i: (0, 0, 0)),
+        in_specs=[anywhere] * 3,
+        out_specs=(anywhere, anywhere),
+        scratch_shapes=[
+            pltpu.VMEM(items, jnp.bfloat16),
+            pltpu.VMEM(prefix_keys.shape, jnp.bfloat16),
+            pltpu.VMEM(prefix_values.shape, jnp.bfloat16),
+            pltpu.VMEM(items, jnp.bfloat16),
+            pltpu.VMEM(lses, jnp.float32),
+            pltpu.SemaphoreType.DMA((2, steps)),
+            pltpu.SemaphoreType.DMA((3,)),
+            pltpu.SemaphoreType.DMA((steps, owners)),
+            pltpu.SemaphoreType.DMA((steps, owners)),
+            pltpu.SemaphoreType.DMA((steps, owners)),
+            pltpu.SemaphoreType.DMA((steps, owners)),
+            pltpu.SemaphoreType.DMA((owners,)),
+            pltpu.SemaphoreType.DMA((owners,)),
+        ],
+        compiler_params=pltpu.CompilerParams(
+            collective_id=0, has_side_effects=True, vmem_limit_bytes=VMEM_LIMIT
         ),
-        compiler_params=params,
         name="span_attention",
-    )(received.reshape(owners, slots, CAP, HEADS, HEAD_DIM), prefix_keys, prefix_values)
-    part_lse = (
-        part_lse.reshape(slots, owners, CAP, HEAD_DIM)
-        .transpose(1, 0, 2, 3)
-        .reshape(owners, slots * CAP, HEAD_DIM)
-    )
-    back_lse = lax.all_to_all(part_lse, "owner", split_axis=0, concat_axis=0, tiled=True)
-    back_out = lax.all_to_all(
-        part_out.reshape(buffer, HEADS, HEAD_DIM), "owner", split_axis=0, concat_axis=0, tiled=True
-    )
+    )(outgoing.reshape(items), prefix_keys, prefix_values)
 
     tokens = rows * suffix_keys.shape[1]
     head_rows = pl.BlockSpec((rows, heads, HEAD_DIM), lambda i: (0, i, 0))
@@ -244,7 +369,7 @@
             suffix_spec,
             suffix_spec,
             pl.BlockSpec((buffer, heads, HEAD_DIM), lambda i: (0, i, 0)),
-            pl.BlockSpec((buffer, HEAD_DIM), lambda i: (0, 0)),
+            pl.BlockSpec((buffer, 1, HEAD_DIM), lambda i: (0, 0, 0)),
         ],
         out_specs=head_rows,
         scratch_shapes=[
@@ -261,8 +386,8 @@
         q3,
         suffix_keys.reshape(tokens, width),
         suffix_values.reshape(tokens, width),
-        back_out,
-        back_lse.reshape(buffer, HEAD_DIM),
+        back_out.reshape(buffer, HEADS, HEAD_DIM),
+        back_lse.reshape(buffer, 1, HEAD_DIM),
     )
     return out.reshape(rows, HEADS * HEAD_DIM)
 

time: 90 us -> 64.2 us (0.71)
  blocking collectives: 70.9 us -> 0 us
  Pallas kernels: 15.3 us -> 60.8 us
    all_to_all x3 -> x0, blocking collectives: 70.9 us -> none  [the longest x1 32 us: body(): lax.all_to_all(outgoing, 'owner', split_axis=0, concat_axis=0, tiled=True)]
    pallas_call x1, Pallas kernels: 10.6 us -> 56.1 us  [body(): pl.pallas_call(functools.partial(span_kernel, chunk=chunk), out_shape=(ja...]
    unnamed x16 -> x12, local copies, waits for them, and re-layouts: 3.19 us -> 3.19 us
where the time goes in v3:
time: 64.2 us; the launch traced here: 64.1 us
  Pallas kernels  60.8 us (95%)
  local copies, waits for them, and re-layouts  3.19 us (5%)
    pallas_call x1, Pallas kernels, body(): pl.pallas_call(functools.partial(span_kernel, chunk=chunk), out_shape=(ja...  56.1 us
    pallas_call x1, Pallas kernels, body(): pl.pallas_call(finish_kernel, grid=(steps,), out_shape=jax.ShapeDtypeStru...  3.96 us
    unnamed x12, local copies, waits for them, and re-layouts  3.19 us

profile of v3, /device:TPU:0, one launch (start us, length us, event | category | flops | bytes accessed | tf_op | source)
XLA Modules:
  0.0 64.1 jit_solution(16636732436070886088)
XLA Ops:
  0.0 1.0 %copy.9 = bf16[2,8,64,128]{3,2,1,0:T(8,128)(2,1)S(1)} copy(bf16[2,8,64,128]{3,1,2,0:T(8,128)(2,1)} %bitcast.22) | data formatting | bytes 524288
  1.0 0.0 copy-start.2
  1.0 0.6 %copy-done.2 = s32[16,1]{0,1:T(1,128)S(1)} copy-done((s32[16,1]{0,1:T(1,128)S(1)}, s32[16,1]{0,1:T(1,128)}, u32[]{:S(2)}) %copy-start.2) | copy-done | bytes 88
  1.7 0.0 copy-start.3
  1.7 0.7 %copy-done.3 = s32[32]{0:T(128)S(1)} copy-done((s32[32]{0:T(128)S(1)}, s32[32]{0:T(128)}, u32[]{:S(2)}) %copy-start.3) | copy-done | bytes 152
  2.3 0.8 %dispatch.1 = bf16[64,64,128]{2,1,0:T(8,128)(2,1)S(1)} custom-call(s32[16]{0:T(128)S(1)} %bitcast.20, s32[32]{0:T(128)S(1)} %copy-done.3, bf16[16,64,128]{2,1,0:T(8,128)(2,1)S(1)} %bitcast.13), custom_call_target="tpu_custom_call" | custom-call | tf_op jit(solution)/shard_map/dispatch/pallas_call | solution.py:315
  3.1 0.0 copy-start
  3.1 0.0 copy-start.1
  3.1 0.0 copy-start.4
  3.1 56.1 %span_attention.1 = (bf16[16,2,2,64,128]{4,3,2,1,0:T(8,128)(2,1)S(1)}, f32[16,2,2,1,128]{4,3,2,1,0:T(1,128)S(1)}) custom-call(bf16[16,2,2,64,128]{4,3,2,1,0:T(8,128)(2,1)S(1)} %bitcast.12, bf16[2,1024,1024]{2,1,0:T(8,128)(2,1)} %k_hbm.1, bf16[2,1024,1024]{2,1,0:T(8,128)(2,1)} %v_hbm.1), custom_call_target="tpu_custom_call" | custom-call | tf_op jit(solution)/shard_map/span_attention/pallas_call | solution.py:328
  59.2 0.0 copy-done
  59.2 0.0 copy-done.1
  59.2 0.0 copy-done.4
  59.2 4.0 %suffix_combine.1 = bf16[16,64,128]{2,1,0:T(8,128)(2,1)S(1)} custom-call(s32[16]{0:T(128)S(1)} %bitcast.21, s32[32]{0:T(128)S(1)} %copy-done.3, s32[16]{0:T(128)S(1)} %copy-done.4, bf16[16,64,128]{2,1,0:T(8,128)(2,1)S(1)} %bitcast.14, bf16[512,1024]{1,0:T(8,128)(2,1)S(1)} %bitcast.15, bf16[512,1024]{1,0:T(8,128)(2,1)S(1)} %bitcast.16, ...), custom_call_target="tpu_custom_call" | custom-call | tf_op jit(solution)/shard_map/suffix_combine/pallas_call | solution.py:360
  63.2 0.9 %copy.12 = bf16[2,8,64,128]{3,1,2,0:T(8,128)(2,1)} copy(bf16[2,8,64,128]{3,2,1,0:T(8,128)(2,1)S(1)} %bitcast.18) | data formatting | bytes 524288
Async XLA Ops:
  1.0 0.7 %copy-start.2 = (s32[16,1]{0,1:T(1,128)S(1)}, s32[16,1]{0,1:T(1,128)}, u32[]{:S(2)}) copy-start(s32[16,1]{0,1:T(1,128)} %param.9) | copy-start | bytes 196
  1.7 0.7 %copy-start.3 = (s32[32]{0:T(128)S(1)}, s32[32]{0:T(128)}, u32[]{:S(2)}) copy-start(s32[32]{0:T(128)} %map_ref.3) | copy-start | bytes 388
  3.1 56.1 %copy-start = (bf16[16,32,1024]{2,1,0:T(8,128)(2,1)S(1)}, bf16[16,32,1024]{2,1,0:T(8,128)(2,1)}, u32[]{:S(2)}) copy-start(bf16[16,32,1024]{2,1,0:T(8,128)(2,1)} %param.14) | copy-start | bytes 3145732
  3.1 56.1 %copy-start.1 = (bf16[16,32,1024]{2,1,0:T(8,128)(2,1)S(1)}, bf16[16,32,1024]{2,1,0:T(8,128)(2,1)}, u32[]{:S(2)}) copy-start(bf16[16,32,1024]{2,1,0:T(8,128)(2,1)} %param.15) | copy-start | bytes 3145732
  3.1 56.1 %copy-start.4 = (s32[16]{0:T(128)S(1)}, s32[16]{0:T(128)}, u32[]{:S(2)}) copy-start(s32[16]{0:T(128)} %len_ref.1) | copy-start | bytes 196

commit v4 on v3

--- a/solution.py
+++ b/solution.py
@@ -89,12 +89,48 @@
             )
 
 
+def attend_suffix(len_ref, q_ref, sk_ref, sv_ref, out_ref, lse_ref):
+    rows = q_ref.shape[0]
+    tokens = sk_ref.shape[0]
+    room = tokens // rows
+    col = lax.broadcasted_iota(jnp.int32, (1, tokens), 1)
+    limit = jnp.zeros((1, tokens), jnp.int32)
+    for r in range(rows):
+        limit = jnp.where(col // room == r, r * room + len_ref[r], limit)
+    owner_row = lax.broadcasted_iota(jnp.int32, (rows * GROUP, tokens), 0) // GROUP
+    visible = (owner_row == col // room) & (col < limit)
+    q = q_ref[...].astype(jnp.float32)
+    for j in range(KV_HEADS):
+        cols = slice(j * HEAD_DIM, (j + 1) * HEAD_DIM)
+        part = slice(j * GROUP, (j + 1) * GROUP)
+        qj = q[:, part].reshape(rows * GROUP, HEAD_DIM).astype(jnp.bfloat16)
+        raw = lax.dot_general(
+            qj, sk_ref[:, cols], (((1,), (1,)), ((), ())), preferred_element_type=jnp.float32
+        )
+        raw = jnp.where(visible, raw, NEG_FILL)
+        highest = jnp.max(raw, axis=-1, keepdims=True)
+        expon = jnp.where(visible, jnp.exp2((raw - highest) * (FACTOR * LOG2E)), 0.0)
+        total = jnp.sum(expon, axis=-1, keepdims=True)
+        mixed = jnp.dot(
+            expon.astype(jnp.bfloat16), sv_ref[:, cols], preferred_element_type=jnp.float32
+        )
+        out_ref[:, part] = (mixed / total).reshape(rows, GROUP, HEAD_DIM)
+        lse = jnp.broadcast_to(highest * FACTOR + jnp.log(total), (rows * GROUP, HEAD_DIM))
+        lse_ref[:, part] = lse.reshape(rows, GROUP, HEAD_DIM)
+
+
 def span_kernel(
     ask_ref,
     k_hbm,
     v_hbm,
+    len_ref,
+    own_q_ref,
+    sk_ref,
+    sv_ref,
     back_ref,
     back_lse_ref,
+    suf_ref,
+    suf_lse_ref,
     q_ref,
     k_ref,
     v_ref,
@@ -186,6 +222,7 @@
         for copy in load(step):
             copy.start()
 
+    attend_suffix(len_ref, own_q_ref, sk_ref, sv_ref, suf_ref, suf_lse_ref)
     own_ask.wait()
 
     @pl.loop(0, steps)
@@ -218,10 +255,8 @@
 def finish_kernel(
     prefix_ref,
     map_ref,
-    len_ref,
-    q_ref,
-    sk_ref,
-    sv_ref,
+    suf_ref,
+    suf_lse_ref,
     back_ref,
     lse_ref,
     out_ref,
@@ -230,11 +265,9 @@
     sel_lse_ref,
 ):
     step = pl.program_id(0)
-    rows = q_ref.shape[0]
+    rows = suf_ref.shape[0]
     per_prefix = map_ref.shape[0] // PREFIXES
     heads = PAIR * GROUP
-    tokens = sk_ref.shape[0]
-    room = tokens // rows
 
     def visit(r, c, pos):
         sel_ref[c, r] = back_ref[pos]
@@ -242,32 +275,12 @@
 
     row_positions(prefix_ref, map_ref, count_ref, rows, per_prefix, visit)
 
-    col = lax.broadcasted_iota(jnp.int32, (1, tokens), 1)
-    limit = jnp.zeros((1, tokens), jnp.int32)
-    for r in range(rows):
-        limit = jnp.where(col // room == r, r * room + len_ref[r], limit)
-    owner_row = lax.broadcasted_iota(jnp.int32, (rows * GROUP, tokens), 0) // GROUP
-    visible = (owner_row == col // room) & (col < limit)
-    q = q_ref[...].astype(jnp.float32)
     results = []
     lane = lax.broadcasted_iota(jnp.int32, (rows, GROUP, HEAD_DIM), 2)
     within = lax.broadcasted_iota(jnp.int32, (rows, GROUP, HEAD_DIM), 1)
     for j in range(PAIR):
-        cols = slice(j * HEAD_DIM, (j + 1) * HEAD_DIM)
         part = slice(j * GROUP, (j + 1) * GROUP)
-        qj = q[:, part].reshape(rows * GROUP, HEAD_DIM).astype(jnp.bfloat16)
-        raw = lax.dot_general(
-            qj, sk_ref[:, cols], (((1,), (1,)), ((), ())), preferred_element_type=jnp.float32
-        )
-        raw = jnp.where(visible, raw, NEG_FILL)
-        highest = jnp.max(raw, axis=-1, keepdims=True)
-        expon = jnp.where(visible, jnp.exp2((raw - highest) * (FACTOR * LOG2E)), 0.0)
-        total = jnp.sum(expon, axis=-1, keepdims=True)
-        mixed = jnp.dot(
-            expon.astype(jnp.bfloat16), sv_ref[:, cols], preferred_element_type=jnp.float32
-        )
-        suffix_out = (mixed / total).reshape(rows, GROUP, HEAD_DIM)
-        suffix_lse = (highest * FACTOR + jnp.log(total)).reshape(rows, GROUP, 1)
+        suffix_out, suffix_lse = suf_ref[:, part], suf_lse_ref[:, part]
         mine = lane == within + (step * heads + j * GROUP)
         span_lse = []
         top = suffix_lse
@@ -305,7 +318,6 @@
     buffer = slot_count * CAP
     heads = PAIR * GROUP
     steps = HEADS // heads
-    cols = PAIR * HEAD_DIM
     params = pltpu.CompilerParams(vmem_limit_bytes=VMEM_LIMIT)
     smem = pl.BlockSpec(memory_space=pltpu.SMEM)
     vmem = pl.BlockSpec(memory_space=pltpu.VMEM)
@@ -325,14 +337,18 @@
     items = (owners, slots, CAP, HEADS, HEAD_DIM)
     lses = (owners, slots, CAP, 1, HEAD_DIM)
     anywhere = pl.BlockSpec(memory_space=pl.ANY)
-    back_out, back_lse = pl.pallas_call(
+    tokens = rows * suffix_keys.shape[1]
+    suffix = jax.ShapeDtypeStruct((rows, HEADS, HEAD_DIM), jnp.float32)
+    back_out, back_lse, suf_out, suf_lse = pl.pallas_call(
         functools.partial(span_kernel, chunk=chunk),
         out_shape=(
             jax.ShapeDtypeStruct(items, jnp.bfloat16),
             jax.ShapeDtypeStruct(lses, jnp.float32),
+            suffix,
+            suffix,
         ),
-        in_specs=[anywhere] * 3,
-        out_specs=(anywhere, anywhere),
+        in_specs=[anywhere] * 3 + [smem, vmem, vmem, vmem],
+        out_specs=(anywhere, anywhere, vmem, vmem),
         scratch_shapes=[
             pltpu.VMEM(items, jnp.bfloat16),
             pltpu.VMEM(prefix_keys.shape, jnp.bfloat16),
@@ -352,11 +368,17 @@
             collective_id=0, has_side_effects=True, vmem_limit_bytes=VMEM_LIMIT
         ),
         name="span_attention",
-    )(outgoing.reshape(items), prefix_keys, prefix_values)
-
-    tokens = rows * suffix_keys.shape[1]
+    )(
+        outgoing.reshape(items),
+        prefix_keys,
+        prefix_values,
+        suffix_len,
+        q3,
+        suffix_keys.reshape(tokens, width),
+        suffix_values.reshape(tokens, width),
+    )
+
     head_rows = pl.BlockSpec((rows, heads, HEAD_DIM), lambda i: (0, i, 0))
-    suffix_spec = pl.BlockSpec((tokens, cols), lambda i: (0, i))
     out = pl.pallas_call(
         finish_kernel,
         grid=(steps,),
@@ -364,10 +386,8 @@
         in_specs=[
             smem,
             smem,
-            smem,
             head_rows,
-            suffix_spec,
-            suffix_spec,
+            head_rows,
             pl.BlockSpec((buffer, heads, HEAD_DIM), lambda i: (0, i, 0)),
             pl.BlockSpec((buffer, 1, HEAD_DIM), lambda i: (0, 0, 0)),
         ],
@@ -382,10 +402,8 @@
     )(
         prefix_ids,
         block_map,
-        suffix_len,
-        q3,
-        suffix_keys.reshape(tokens, width),
-        suffix_values.reshape(tokens, width),
+        suf_out,
+        suf_lse,
         back_out.reshape(buffer, HEADS, HEAD_DIM),
         back_lse.reshape(buffer, 1, HEAD_DIM),
     )

time: 64.2 us -> 65.8 us (1.025)
  local copies, waits for them, and re-layouts: 3.19 us -> 6.27 us
  Pallas kernels: 60.8 us -> 59.2 us
    unnamed x12, local copies, waits for them, and re-layouts: 3.19 us -> 6.27 us
    pallas_call x1, Pallas kernels: 3.96 us -> 1.87 us  [body(): pl.pallas_call(finish_kernel, grid=(steps,), out_shape=jax.ShapeDtypeStru...]
where the time goes in v4:
time: 65.8 us; the launch traced here: 65.5 us
  Pallas kernels  59.2 us (90%)
  local copies, waits for them, and re-layouts  6.27 us (10%)
    pallas_call x1, Pallas kernels, body(): pl.pallas_call(functools.partial(span_kernel, chunk=chunk), out_shape=(ja...  56.6 us
    unnamed x12, local copies, waits for them, and re-layouts  6.27 us
    pallas_call x1, Pallas kernels, body(): pl.pallas_call(finish_kernel, grid=(steps,), out_shape=jax.ShapeDtypeStru...  1.87 us

profile of v4, /device:TPU:0, one launch (start us, length us, event | category | flops | bytes accessed | tf_op | source)
XLA Modules:
  0.0 65.5 jit_solution(3521375437619653614)
XLA Ops:
  0.0 1.0 %copy.9 = bf16[2,8,64,128]{3,2,1,0:T(8,128)(2,1)S(1)} copy(bf16[2,8,64,128]{3,1,2,0:T(8,128)(2,1)} %bitcast.22) | data formatting | bytes 524288
  1.0 0.0 copy-start.2
  1.0 0.6 copy-done.2
  1.7 0.0 copy-start.3
  1.7 0.7 copy-done.3
  2.3 0.8 %dispatch.1 = bf16[64,64,128]{2,1,0:T(8,128)(2,1)S(1)} custom-call(s32[16]{0:T(128)S(1)} %bitcast.20, s32[32]{0:T(128)S(1)} %copy-done.3, bf16[16,64,128]{2,1,0:T(8,128)(2,1)S(1)} %bitcast.13), custom_call_target="tpu_custom_call" | custom-call | tf_op jit(solution)/shard_map/dispatch/pallas_call | solution.py:327
  3.1 0.0 copy-start
  3.1 1.2 %copy-done = bf16[16,32,1024]{2,1,0:T(8,128)(2,1)S(1)} copy-done((bf16[16,32,1024]{2,1,0:T(8,128)(2,1)S(1)}, bf16[16,32,1024]{2,1,0:T(8,128)(2,1)}, u32[]{:S(2)}) %copy-start) | copy-done | bytes 1048600
  4.3 0.0 copy-start.1
  4.3 1.2 %copy-done.1 = bf16[16,32,1024]{2,1,0:T(8,128)(2,1)S(1)} copy-done((bf16[16,32,1024]{2,1,0:T(8,128)(2,1)S(1)}, bf16[16,32,1024]{2,1,0:T(8,128)(2,1)}, u32[]{:S(2)}) %copy-start.1) | copy-done | bytes 1048600
  5.5 0.0 copy-start.4
  5.5 0.7 copy-done.4
  6.2 56.6 %span_attention.1 = (bf16[16,2,2,64,128]{4,3,2,1,0:T(8,128)(2,1)S(1)}, f32[16,2,2,1,128]{4,3,2,1,0:T(1,128)S(1)}, f32[16,64,128]{2,1,0:T(8,128)S(1)}, f32[16,64,128]{2,1,0:T(8,128)S(1)}) custom-call(bf16[16,2,2,64,128]{4,3,2,1,0:T(8,128)(2,1)S(1)} %bitcast.12, bf16[2,1024,1024]{2,1,0:T(8,128)(2,1)} %k_hbm.1, bf16[2,1024,1024]{2,1,0:T(8,128)(2,1)} %v_hbm.1, ...), custom_call_target="tpu_custom_call" | custom-call | tf_op jit(solution)/shard_map/span_attention/pallas_call | solution.py:342
  62.8 1.9 %suffix_combine.1 = bf16[16,64,128]{2,1,0:T(8,128)(2,1)S(1)} custom-call(s32[16]{0:T(128)S(1)} %bitcast.21, s32[32]{0:T(128)S(1)} %copy-done.3, f32[16,64,128]{2,1,0:T(8,128)S(1)} %get-tuple-element.9.suf_ref, f32[16,64,128]{2,1,0:T(8,128)S(1)} %get-tuple-element.10.suf_lse_ref, bf16[64,64,128]{2,1,0:T(8,128)(2,1)S(1)} %bitcast.18, f32[64,1,128]{2,1,0:T(1,128)S(1)} %bitcast.19), custom_call_target="tpu_custom_call" | custom-call | tf_op jit(solution)/shard_map/suffix_combine/pallas_call | solution.py:382
  64.7 0.9 %copy.12 = bf16[2,8,64,128]{3,1,2,0:T(8,128)(2,1)} copy(bf16[2,8,64,128]{3,2,1,0:T(8,128)(2,1)S(1)} %bitcast.17) | data formatting | bytes 524288
Async XLA Ops:
  1.0 0.7 %copy-start.2 = (s32[16,1]{0,1:T(1,128)S(1)}, s32[16,1]{0,1:T(1,128)}, u32[]{:S(2)}) copy-start(s32[16,1]{0,1:T(1,128)} %param.9) | copy-start | bytes 196
  1.7 0.7 copy-start.3
  3.1 1.2 %copy-start = (bf16[16,32,1024]{2,1,0:T(8,128)(2,1)S(1)}, bf16[16,32,1024]{2,1,0:T(8,128)(2,1)}, u32[]{:S(2)}) copy-start(bf16[16,32,1024]{2,1,0:T(8,128)(2,1)} %param.14) | copy-start | bytes 3145732
  4.3 1.2 %copy-start.1 = (bf16[16,32,1024]{2,1,0:T(8,128)(2,1)S(1)}, bf16[16,32,1024]{2,1,0:T(8,128)(2,1)}, u32[]{:S(2)}) copy-start(bf16[16,32,1024]{2,1,0:T(8,128)(2,1)} %param.15) | copy-start | bytes 3145732
  5.5 0.7 copy-start.4
